TPU v7x, 256 devices: a whole 4x4x8 slice. The times are simulated.
256 devices in a mesh: fit: 32 (over x, y, core), batch: 8 (over z).
Axes of the slice: x: 4, y: 4, z: 8, core: 2. Of those that a mesh axis runs over, the one named last changes fastest.
Arguments:
- half_ints: bfloat16 [30720, 384, 128], P('fit', 'batch')
- domain_tiles: int32 [256, 6], P('batch'), may hold values from 0 to 7, as said below
- tile_counts: int32 [256, 6], P('batch'), may hold values from 0 to 128, as said below
Outputs:
- exchange_k: float32 [1024, 1024], P('fit', 'batch')
Inputs may be any that keep to these rules, and one draw needn't show every extreme that they name: `tile_counts`: in each orbital the slots with a count above 0 come first. In every group of 32 orbitals there are 48 such slots: exactly one orbital has 6, 11 others have 2, the rest 1, so that the squared numbers sum to 100. Every live slot but an orbital's last holds 128 valid functions. `domain_tiles`: the tiles of one orbital differ.
All inputs are finite; a program needn't handle non-finite values.
Results may differ from a plain program's by a relative error of at most 0.0003.
Values sent between devices are 32-bit elements; how exact they have to be, the bound alone decides.
No kernel may reach another device: no remote copies, remote signals or barrier semaphores. Data moves between devices by JAX's collectives and lax.ppermute only.
A program may use at most 192 MiB of HBM per device.

v0:
```python
import jax
import jax.numpy as jnp
from jax import lax
from jax.experimental import pallas as pl
from jax.experimental.pallas import tpu as pltpu
from jax.sharding import PartitionSpec as P

TILE = 128
TILES = 8
MAXT = 6
ORBITALS = 32
SLOTS = 48
DOUBLES = 11
SINGLES = 20
CHUNKS = 15
CORES = 2
RING = 4
HALF = TILE // 2
STRIP = 32
BLOCKS = 16
DIAGONALS = TILES // 2
EIGHT = EXTRA = 8
SHARE = BLOCKS * STRIP + EXTRA


def tn_dot(a, b):
    return lax.dot_general(a, b, (((0,), (0,)), ((), ())), preferred_element_type=jnp.float32)


def left_lanes(shape):
    return lax.broadcasted_iota(jnp.int32, shape, len(shape) - 1) < HALF


def same_index(low, high, odd):
    if isinstance(odd, int):
        m, n = low >> 1, high >> 1
        if odd:
            return (n * 4 + m) if low & 1 else (m * 4 + n)
        return 12 + m if m == n else (low & 1) * 6 + m * 3 - m * (m - 1) // 2 + n - m - 1
    m, n = low >> 1, high >> 1
    mixed = jnp.where((low & 1) == 1, n * 4 + m, m * 4 + n)
    alike = (low & 1) * 6 + m * 3 - ((m * (m - 1)) >> 1) + n - m - 1
    return jnp.where(odd == 1, mixed, jnp.where(m == n, 12 + m, alike))


def cross_pair(k, index):
    if k == 0:
        m = index % 4
        return (2 * m, 2 * m + 1) if index < 4 else (2 * m, 2 * m)
    m = [m for m in range(RING) if m < m ^ k][index // 4]
    return 2 * m + (index // 2) % 2, 2 * (m ^ k) + index % 2


def place():
    fit = lax.axis_index("fit")
    return fit // (RING * CORES), lax.rem(fit // CORES, RING), lax.rem(fit, CORES)


def gram_kernel(
    slots_hbm, x_hbm, out_ref,
    raw, slots, same, cross, ones, twos, six, legs, slots_ref, load_sem, index_sem,
):
    rows = raw.shape[0] // CHUNKS

    def load(i):
        part = pl.ds(i * rows, rows)
        return pltpu.make_async_copy(x_hbm.at[part], raw.at[part], load_sem.at[i])

    load_slots = pltpu.make_async_copy(slots_hbm, slots_ref, index_sem)
    load_slots.start()
    for i in range(CHUNKS):
        load(i).start()
    same[...] = jnp.zeros_like(same)
    cross[...] = jnp.zeros_like(cross)
    out_ref[...] = jnp.zeros_like(out_ref)

    x, y, core = place()
    for owner, here in enumerate((y, x)):
        for there in range(RING):
            legs[owner * RING + there] = ((owner ^ core) * RING + ((there - here) & (RING - 1))) * (SHARE // EIGHT)

    load_slots.wait()

    def tile(k, i):
        return slots_ref[k, i] >> 8

    def count(k, i):
        return slots_ref[k, i] & 255

    offset = n_one = n_two = six_at = six_offset = jnp.int32(0)
    for i in range(ORBITALS):
        last = count(1, i)
        more = (last > 0).astype(jnp.int32)
        many = (count(2, i) > 0).astype(jnp.int32)
        first, second = tile(0, i), tile(1, i)
        ones[0, n_one] = offset
        ones[1, n_one] = first
        ones[2, n_one] = count(0, i)
        ordered = first < second
        twos[0, n_two] = jnp.where(ordered, offset, offset + 1)
        twos[1, n_two] = jnp.where(ordered, offset + 1, offset)
        twos[2, n_two] = jnp.where(ordered, first, second)
        twos[3, n_two] = jnp.where(ordered, second, first)
        twos[4, n_two] = jnp.where(ordered, TILE, last)
        twos[5, n_two] = jnp.where(ordered, last, TILE)
        six_at = six_at + many * i
        six_offset = six_offset + many * offset
        offset = offset + 1 + more + (MAXT - 2) * many
        n_one = n_one + 1 - more
        n_two = n_two + more - many
    for k in range(MAXT):
        rank = jnp.int32(0)
        for l in range(MAXT):
            if l != k:
                rank = rank + (tile(l, six_at) < tile(k, six_at)).astype(jnp.int32)
        six[0, rank] = six_offset + k
        six[1, rank] = tile(k, six_at)
        six[2, rank] = count(k, six_at)

    for i in range(CHUNKS):
        load(i).wait()
        part = pl.ds(i * rows, rows)
        slots[:, part, :] = jnp.swapaxes(raw[part], 0, 1)

    lane = lax.broadcasted_iota(jnp.int32, (1, TILE), 1)

    def masked(column, count):
        return slots[column] * (lane < count).astype(jnp.float32).astype(jnp.bfloat16)

    left = left_lanes((HALF, TILE))

    def add(a, b, gram):
        pair = a * TILES + b
        same[pair] += jnp.where(left, gram[:HALF], gram[HALF:])
        cross[pair] += jnp.where(left, gram[HALF:], gram[:HALF])

    tile_of = [six[1, k] for k in range(MAXT)]
    sides = [masked(six[0, k], six[2, k]) for k in range(MAXT)]
    for pair in range(MAXT // 2):
        gram = tn_dot(jnp.concatenate(sides[:2 * pair + 2], axis=1), jnp.concatenate(sides[2 * pair:2 * pair + 2], axis=1))
        for b in (2 * pair, 2 * pair + 1):
            for a in range(b + 1):
                block = gram[a * TILE:(a + 1) * TILE, (b - 2 * pair) * TILE:(b - 2 * pair + 1) * TILE]
                add(tile_of[a], tile_of[b], block)
    for j in range(DOUBLES):
        both = jnp.concatenate([masked(twos[0, j], twos[4, j]), masked(twos[1, j], twos[5, j])], axis=1)
        gram = tn_dot(both, both)
        low, high = twos[2, j], twos[3, j]
        add(low, low, gram[:TILE, :TILE])
        add(low, high, gram[:TILE, TILE:])
        add(high, high, gram[TILE:, TILE:])
    for j in range(SINGLES):
        only = masked(ones[0, j], ones[2, j])
        add(ones[1, j], ones[1, j], tn_dot(only, only))

    z = lax.axis_index("batch")
    near = left_lanes((STRIP, TILE))
    row_of = lax.broadcasted_iota(jnp.int32, (HALF, TILE), 0)
    col_of = lax.broadcasted_iota(jnp.int32, (HALF, TILE), 1) & (HALF - 1)
    for a in range(TILES):
        for b in range(a, TILES):
            block = same[a * TILES + b]
            if a == b and a % 2 == 1:
                continue
            if a == b:
                beside = same[(a + 1) * (TILES + 1)]
                block = jnp.where(row_of >= col_of, block, beside)
                diagonal = jnp.sum(jnp.where(row_of == col_of, beside, 0.0), axis=0, keepdims=True)
                for i in range(2):
                    out_ref[legs[(z & 1) * 2 + i] + BLOCKS * STRIP // EIGHT, a // 2:a // 2 + 1, :] = diagonal
            top, bottom = block[:STRIP], block[STRIP:]
            first = jnp.where(near, top, pltpu.roll(bottom, HALF, 1))
            second = jnp.where(near, pltpu.roll(top, HALF, 1), bottom)
            odd = (a ^ b) & 1
            index = same_index(a, b, odd)
            for i, value in enumerate((first, second)):
                to_y = ((z & 1) ^ odd) * 2 + i
                rows = pl.ds(legs[to_y] + index * (STRIP // EIGHT), STRIP // EIGHT)
                out_ref[rows] = value.reshape(STRIP // EIGHT, EIGHT, TILE)
    for k in range(RING):
        target = legs[RING + (k ^ (z >> 1))]
        for index in range(TILES):
            a, b = cross_pair(k, index)
            if a == b:
                value = jnp.where(left, cross[(a + 1) * (TILES + 1)], cross[a * (TILES + 1)])
            else:
                value = cross[a * TILES + b]
            rows = pl.ds(target + index * (HALF // EIGHT), HALF // EIGHT)
            out_ref[rows] = value.reshape(HALF // EIGHT, EIGHT, TILE)


def grams(half_ints, domain_tiles, tile_counts):
    fit_rows = half_ints.shape[0]
    hbm = pl.BlockSpec(memory_space=pltpu.HBM)
    return pl.pallas_call(
        gram_kernel,
        in_specs=[hbm, pl.BlockSpec(memory_space=pl.ANY)],
        out_specs=pl.BlockSpec(memory_space=pltpu.VMEM),
        out_shape=jax.ShapeDtypeStruct((CORES * RING * SHARE // EIGHT, EIGHT, TILE), jnp.float32),
        scratch_shapes=[
            pltpu.VMEM((fit_rows, SLOTS, TILE), jnp.bfloat16),
            pltpu.VMEM((SLOTS, fit_rows, TILE), jnp.bfloat16),
            pltpu.VMEM((TILES * TILES, HALF, TILE), jnp.float32),
            pltpu.VMEM((TILES * TILES, HALF, TILE), jnp.float32),
            pltpu.SMEM((3, ORBITALS), jnp.int32),
            pltpu.SMEM((6, ORBITALS), jnp.int32),
            pltpu.SMEM((3, MAXT), jnp.int32),
            pltpu.SMEM((CORES * RING,), jnp.int32),
            pltpu.SMEM((MAXT, ORBITALS), jnp.int32),
            pltpu.SemaphoreType.DMA((CHUNKS,)),
            pltpu.SemaphoreType.DMA,
        ],
        compiler_params=pltpu.CompilerParams(vmem_limit_bytes=48 * 2**20),
        name="grams",
    )((domain_tiles * 256 + tile_counts).T, half_ints)


def ring_moves(step, turn):
    moves = []
    for x in range(RING):
        for y in range(RING):
            for core in range(CORES):
                along_x = core != turn
                to_x = (x + step) % RING if along_x else x
                to_y = y if along_x else (y + step) % RING
                moves.append(((x * RING + y) * CORES + core, (to_x * RING + to_y) * CORES + core))
    return moves


def expand_kernel(own_ref, one_ref, two_ref, three_ref, out_ref, line, blocks):
    line[...] = own_ref[...] + one_ref[...] + two_ref[...] + three_ref[...]
    x, y, core = place()
    z = lax.axis_index("batch")
    near = left_lanes((STRIP, TILE))

    def pack(pair):
        top, bottom = pair[:STRIP], pair[STRIP:]
        return (
            jnp.where(near, top, pltpu.roll(bottom, HALF, 1)),
            jnp.where(near, pltpu.roll(top, HALF, 1), bottom),
        )

    def keep_flipped(pairs, indices):
        turned = jnp.concatenate(pairs, axis=0).T
        flipped = (*pack(turned[:HALF]), *pack(turned[HALF:]))
        for index, value in zip(indices, flipped):
            blocks[BLOCKS + index] = value

    @pl.when(core == 0)
    def _():
        packed = [line[n * STRIP:(n + 1) * STRIP] for n in range(BLOCKS)]
        for n in range(BLOCKS):
            blocks[n] = packed[n]
        pairs = []
        for n in range(0, BLOCKS, 2):
            a, b = packed[n], packed[n + 1]
            top = jnp.where(near, a, pltpu.roll(b, HALF, 1))
            bottom = jnp.where(near, pltpu.roll(a, HALF, 1), b)
            pairs.append(jnp.concatenate([top, bottom], axis=0))
        for n in range(0, BLOCKS, 4):
            keep_flipped(pairs[n // 2:n // 2 + 2], (n, n + 2, n + 1, n + 3))
        odd = (y >> 1) ^ (z & 1)
        row_of = lax.broadcasted_iota(jnp.int32, (STRIP, TILE), 0)
        lane_of = lax.broadcasted_iota(jnp.int32, (STRIP, TILE), 1)
        row_of = row_of + (lane_of // HALF) * STRIP
        col_of = lane_of & (HALF - 1)
        diagonals = line[BLOCKS * STRIP:]
        on_half = (lax.broadcasted_iota(jnp.int32, (EXTRA, TILE), 1) // HALF) == (y & 1)
        diagonals = jnp.where(on_half, diagonals, pltpu.roll(diagonals, HALF, 1))

        @pl.when(odd == 0)
        def _():
            for m in range(DIAGONALS):
                both, turned = blocks[12 + m], blocks[BLOCKS + 12 + m]
                second = jnp.where(row_of < col_of, both, turned)
                blocks[12 + m] = jnp.where(row_of >= col_of, both, turned)
                blocks[BLOCKS + 12 + m] = jnp.where(row_of == col_of, diagonals[m:m + 1], second)

        for to_x in range(RING):
            for col in range(TILES):
                row = 2 * to_x + ((col & 1) ^ odd)
                index = same_index(jnp.minimum(row, col), jnp.maximum(row, col), odd)
                flip = jnp.where(row == col, (row & 1) == 1, row > col)
                out_ref[((to_x - x) & (RING - 1)) * TILES + col] = blocks[jnp.where(flip, index + BLOCKS, index)]

    @pl.when(core == 1)
    def _():
        pairs = [line[n * HALF:(n + 1) * HALF] for n in range(TILES)]
        for n in range(TILES):
            blocks[2 * n], blocks[2 * n + 1] = pack(pairs[n])
        for n in range(0, TILES, 2):
            keep_flipped(pairs[n:n + 2], (2 * n, 2 * n + 2, 2 * n + 1, 2 * n + 3))
        k = x ^ (z >> 1)
        for to_y in range(RING):
            for col in range(TILES):
                row = 2 * ((col >> 1) ^ k) + (to_y >> 1)
                i = to_y & 1
                low, high = jnp.minimum(row, col), jnp.maximum(row, col)
                m = low >> 1
                index = jnp.where(k == 1, m >> 1, m) * 4 + (low & 1) * 2 + (high & 1)
                index = jnp.where(k == 0, jnp.where(row == col, 4 + m, m), index)
                lower_half = jnp.where(row == col, row & 1, jnp.where(row < col, i, 1 - i))
                direct = jnp.where(row == col, (row & 1) == i, row < col)
                index = index * 2 + 1 - lower_half
                out_ref[((to_y - y) & (RING - 1)) * TILES + col] = blocks[jnp.where(direct, index, index + BLOCKS)]


def expand(*pieces):
    vmem = pl.BlockSpec(memory_space=pltpu.VMEM)
    return pl.pallas_call(
        expand_kernel,
        in_specs=[vmem] * len(pieces),
        out_specs=vmem,
        out_shape=jax.ShapeDtypeStruct((RING * TILES, STRIP, TILE), jnp.float32),
        scratch_shapes=[
            pltpu.VMEM((SHARE, TILE), jnp.float32),
            pltpu.VMEM((2 * BLOCKS, STRIP, TILE), jnp.float32),
        ],
        compiler_params=pltpu.CompilerParams(vmem_limit_bytes=8 * 2**20),
        name="expand",
    )(*pieces)


def last_groups():
    groups = []
    for x in range(RING):
        for odd in range(2):
            for i in range(2):
                groups.append([
                    ((x * RING + ((z & 1) ^ odd) * 2 + i) * CORES) * TILES + z for z in range(TILES)
                ])
    for k in range(RING):
        for y in range(RING):
            groups.append([
                ((((z >> 1) ^ k) * RING + y) * CORES + 1) * TILES + z for z in range(TILES)
            ])
    return groups


def local(half_ints, domain_tiles, tile_counts):
    parts = grams(half_ints, domain_tiles, tile_counts).reshape(CORES, RING, SHARE, TILE)
    keep, send = parts[0], parts[1]
    swap = [(f, f ^ 1) for f in range(RING * RING * CORES)]
    chip = {u: keep[u] + lax.ppermute(send[u], "fit", swap) for u in (2, 1, 3, 0)}
    moved = [lax.ppermute(chip[u], "fit", ring_moves(u, 0)) for u in (2, 1, 3)]
    fit = lax.axis_index("fit")
    core = fit & 1
    column_half = ((fit >> 1) & 1) ^ core
    line = expand(chip[0], *moved).reshape(RING, TILES, STRIP, TILE)
    row = line[0]
    for w in (2, 1, 3):
        row = row + lax.ppermute(line[w], "fit", ring_moves(w, 1))
    row, core, column_half = lax.optimization_barrier((row, core, column_half))
    terms = lax.all_to_all(row, ("fit", "batch"), 0, 0, axis_index_groups=last_groups())
    terms, core, column_half = lax.optimization_barrier((terms, core, column_half))
    mine = jnp.sum(terms, axis=0)
    other = lax.ppermute(mine, "fit", swap)
    at = jnp.arange(TILE, dtype=jnp.int32)[None, :] // HALF
    turned_mine, turned_other = (jnp.roll(block, HALF, axis=1) for block in (mine, other))
    return jnp.where(
        at == column_half,
        jnp.where(core == column_half, mine, turned_mine),
        jnp.where(core == column_half, turned_other, other),
    )


def solution(mesh):
    return jax.shard_map(
        local,
        mesh=mesh,
        in_specs=(P("fit", "batch", None), P("batch", None), P("batch", None)),
        out_specs=P("fit", "batch"),
        check_vma=False,
    )
```

profile of v0, /device:TPU:1, one launch (start us, length us, event | category | flops | bytes accessed | tf_op | source)
XLA Modules:
  0.0 57.1 jit_solution(16281380681383454526)
XLA Ops:
  0.0 0.7 %add_bitcast_fusion.slots_hbm = s32[6,32]{1,0:T(8,128)S(1)} fusion(s32[32,6]{0,1:T(8,128)} %param.5, s32[32,6]{0,1:T(8,128)} %param.4), kind=kLoop, calls=%fused_computation.18 | loop fusion | flops 384 | bytes 2304 | tf_op jit(solution)/shard_map/transpose | solution.py:215
  0.7 9.6 %grams.1 = f32[520,8,128]{2,1,0:T(8,128)S(1)} custom-call(s32[6,32]{1,0:T(8,128)S(1)} %add_bitcast_fusion.slots_hbm, bf16[960,48,128]{2,1,0:T(8,128)(2,1)} %x_hbm.1), custom_call_target="tpu_custom_call" | custom-call | tf_op jit(solution)/shard_map/grams/pallas_call | solution.py:195
  10.3 0.1 slice_bitcast_fusion
  10.4 3.3 %collective-permute-start = (f32[520,128]{1,0:T(8,128)S(1)}, f32[520,128]{1,0:T(8,128)S(1)}, u32[]{:S(2)}, u32[]{:S(2)}) collective-permute-start(f32[520,128]{1,0:T(8,128)S(1)} %get-tuple-element.24), channel_id=1, source_target_pairs={{0,8},{8,0},{16,24},{24,16},{32,40},{40,32},{48,56},{56,48},{64,72... | collective-permute-start | bytes 798728 | tf_op jit(solution)/shard_map/ppermute | solution.py:344
  13.7 0.1 collective-permute-start.1
  13.8 0.4 collective-permute-start.3
  14.2 0.1 collective-permute-start.5
  14.3 0.6 collective-permute-done
  14.9 0.4 collective-permute-done.1
  15.3 0.4 collective-permute-done.3
  15.6 0.4 collective-permute-done.5
  16.0 0.2 fusion
  16.2 1.3 %collective-permute-start.2 = (f32[520,128]{1,0:T(8,128)S(1)}, f32[520,128]{1,0:T(8,128)S(1)}, u32[]{:S(2)}, u32[]{:S(2)}) collective-permute-start(f32[520,128]{1,0:T(8,128)S(1)} %get-tuple-element.19), channel_id=1, source_target_pairs={{0,32},{8,136},{16,48},{24,152},{32,0},{40,168},{48,16},{56,184},{... | collective-permute-start | bytes 798728 | tf_op jit(solution)/shard_map/ppermute | solution.py:345
  17.5 0.3 collective-permute-start.4
  17.8 2.4 %collective-permute-start.6 = (f32[520,128]{1,0:T(8,128)S(1)}, f32[520,128]{1,0:T(8,128)S(1)}, u32[]{:S(2)}, u32[]{:S(2)}) collective-permute-start(f32[520,128]{1,0:T(8,128)S(1)} %get-tuple-element.17), channel_id=1, source_target_pairs={{0,48},{8,200},{16,0},{24,216},{32,16},{40,232},{48,32},{56,248},{... | collective-permute-start | bytes 798728 | tf_op jit(solution)/shard_map/ppermute | solution.py:345
  20.1 3.4 %collective-permute-done.2.one_ref = f32[520,128]{1,0:T(8,128)S(1)} collective-permute-done((f32[520,128]{1,0:T(8,128)S(1)}, f32[520,128]{1,0:T(8,128)S(1)}, u32[]{:S(2)}, u32[]{:S(2)}) %collective-permute-start.2) | collective-permute-done | bytes 266272 | tf_op jit(solution)/shard_map/ppermute | solution.py:345
  23.5 2.8 %collective-permute-done.4.two_ref = f32[520,128]{1,0:T(8,128)S(1)} collective-permute-done((f32[520,128]{1,0:T(8,128)S(1)}, f32[520,128]{1,0:T(8,128)S(1)}, u32[]{:S(2)}, u32[]{:S(2)}) %collective-permute-start.4) | collective-permute-done | bytes 266272 | tf_op jit(solution)/shard_map/ppermute | solution.py:345
  26.4 0.0 collective-permute-done.6.three_ref
  26.4 0.5 expand.1
  26.9 1.3 %collective-permute-start.7 = (f32[8,32,128]{2,1,0:T(8,128)S(1)}, f32[8,32,128]{2,1,0:T(8,128)S(1)}, u32[]{:S(2)}, u32[]{:S(2)}) collective-permute-start(f32[8,32,128]{2,1,0:T(8,128)S(1)} %get-tuple-element.25), channel_id=1, source_target_pairs={{0,128},{8,40},{16,144},{24,56},{32,160},{40,8},{48,176},{56,24},{... | collective-permute-start | bytes 393224 | tf_op jit(solution)/shard_map/ppermute | solution.py:352
  28.3 0.4 collective-permute-start.8
  28.7 2.3 %collective-permute-start.9 = (f32[8,32,128]{2,1,0:T(8,128)S(1)}, f32[8,32,128]{2,1,0:T(8,128)S(1)}, u32[]{:S(2)}, u32[]{:S(2)}) collective-permute-start(f32[8,32,128]{2,1,0:T(8,128)S(1)} %get-tuple-element.26), channel_id=1, source_target_pairs={{0,192},{8,56},{16,208},{24,8},{32,224},{40,24},{48,240},{56,40},{... | collective-permute-start | bytes 393224 | tf_op jit(solution)/shard_map/ppermute | solution.py:352
  30.9 1.4 %collective-permute-done.7 = f32[8,32,128]{2,1,0:T(8,128)S(1)} collective-permute-done((f32[8,32,128]{2,1,0:T(8,128)S(1)}, f32[8,32,128]{2,1,0:T(8,128)S(1)}, u32[]{:S(2)}, u32[]{:S(2)}) %collective-permute-start.7) | collective-permute-done | bytes 131104 | tf_op jit(solution)/shard_map/ppermute | solution.py:352
  32.4 1.7 %collective-permute-done.8 = f32[8,32,128]{2,1,0:T(8,128)S(1)} collective-permute-done((f32[8,32,128]{2,1,0:T(8,128)S(1)}, f32[8,32,128]{2,1,0:T(8,128)S(1)}, u32[]{:S(2)}, u32[]{:S(2)}) %collective-permute-start.8) | collective-permute-done | bytes 131104 | tf_op jit(solution)/shard_map/ppermute | solution.py:352
  34.0 0.0 collective-permute-done.9
  34.1 19.1 %all_to_all.5 = f32[8,32,128]{2,1,0:T(8,128)S(1)} all-to-all(f32[8,32,128]{2,1,0:T(8,128)S(1)} %fusion.5), channel_id=1, replica_groups={{0,33,2,35,4,37,6,39},{16,49,18,51,20,53,22,55},{32,1,34,3,36,5,38,7},{..., dimensions={0} | all-to-all | bytes 262144 | tf_op jit(solution)/shard_map/all_to_all | solution.py:354
  53.2 2.3 %collective-permute-start.10 = (f32[32,128]{1,0:T(8,128)S(1)}, f32[32,128]{1,0:T(8,128)S(1)}, u32[]{:S(2)}, u32[]{:S(2)}) collective-permute-start(f32[32,128]{1,0:T(8,128)S(1)} %reduce_sum.9), channel_id=1, source_target_pairs={{0,8},{8,0},{16,24},{24,16},{32,40},{40,32},{48,56},{56,48},{64,72... | collective-permute-start | bytes 49160 | tf_op jit(solution)/shard_map/ppermute | solution.py:357
  55.5 0.1 fusion.10
  55.6 0.8 %collective-permute-done.10 = f32[32,128]{1,0:T(8,128)S(1)} collective-permute-done((f32[32,128]{1,0:T(8,128)S(1)}, f32[32,128]{1,0:T(8,128)S(1)}, u32[]{:S(2)}, u32[]{:S(2)}) %collective-permute-start.10) | collective-permute-done | bytes 16416 | tf_op jit(solution)/shard_map/ppermute | solution.py:357
  56.3 0.1 fusion.9
  56.4 0.7 %fusion.6 = f32[32,128]{1,0:T(8,128)} fusion(f32[32,128]{1,0:T(8,128)S(1)} %reduce_sum.9, f32[32,64]{1,0:T(8,128)S(1)} %get-tuple-element.31, f32[32,64]{1,0:T(8,128)S(1)} %get-tuple-element.30, f32[32,128]{1,0:T(8,128)S(1)} %collective-permute-done.10, f32[32,64]{1,0:T(8,128)S(1)} %get-tuple-element.29, f32[32,64]{1,0:T(8,128)S(1)} %get-tuple-element.28, ...), kind=kLoop, calls=%fused_computation.16 | loop fusion | flops 20480 | bytes 82049 | tf_op jit(solution)/shard_map/jit(_where)/select_n | solution.py:360
  (4 shorter events, 0.1 us)
Async XLA Ops:
  10.4 4.5 %collective-permute-start = (f32[520,128]{1,0:T(8,128)S(1)}, f32[520,128]{1,0:T(8,128)S(1)}, u32[]{:S(2)}, u32[]{:S(2)}) collective-permute-start(f32[520,128]{1,0:T(8,128)S(1)} %get-tuple-element.24), channel_id=1, source_target_pairs={{0,8},{8,0},{16,24},{24,16},{32,40},{40,32},{48,56},{56,48},{64,72... | collective-permute-start | bytes 798728 | tf_op jit(solution)/shard_map/ppermute | solution.py:344
  13.7 1.5 %collective-permute-start.1 = (f32[520,128]{1,0:T(8,128)S(1)}, f32[520,128]{1,0:T(8,128)S(1)}, u32[]{:S(2)}, u32[]{:S(2)}) collective-permute-start(f32[520,128]{1,0:T(8,128)S(1)} %get-tuple-element.23), channel_id=1, source_target_pairs={{0,8},{8,0},{16,24},{24,16},{32,40},{40,32},{48,56},{56,48},{64,72... | collective-permute-start | bytes 798728 | tf_op jit(solution)/shard_map/ppermute | solution.py:344
  13.8 1.8 %collective-permute-start.3 = (f32[520,128]{1,0:T(8,128)S(1)}, f32[520,128]{1,0:T(8,128)S(1)}, u32[]{:S(2)}, u32[]{:S(2)}) collective-permute-start(f32[520,128]{1,0:T(8,128)S(1)} %get-tuple-element.22), channel_id=1, source_target_pairs={{0,8},{8,0},{16,24},{24,16},{32,40},{40,32},{48,56},{56,48},{64,72... | collective-permute-start | bytes 798728 | tf_op jit(solution)/shard_map/ppermute | solution.py:344
  14.2 1.8 %collective-permute-start.5 = (f32[520,128]{1,0:T(8,128)S(1)}, f32[520,128]{1,0:T(8,128)S(1)}, u32[]{:S(2)}, u32[]{:S(2)}) collective-permute-start(f32[520,128]{1,0:T(8,128)S(1)} %get-tuple-element.21), channel_id=1, source_target_pairs={{0,8},{8,0},{16,24},{24,16},{32,40},{40,32},{48,56},{56,48},{64,72... | collective-permute-start | bytes 798728 | tf_op jit(solution)/shard_map/ppermute | solution.py:344
  16.2 7.4 %collective-permute-start.2 = (f32[520,128]{1,0:T(8,128)S(1)}, f32[520,128]{1,0:T(8,128)S(1)}, u32[]{:S(2)}, u32[]{:S(2)}) collective-permute-start(f32[520,128]{1,0:T(8,128)S(1)} %get-tuple-element.19), channel_id=1, source_target_pairs={{0,32},{8,136},{16,48},{24,152},{32,0},{40,168},{48,16},{56,184},{... | collective-permute-start | bytes 798728 | tf_op jit(solution)/shard_map/ppermute | solution.py:345
  17.5 8.9 %collective-permute-start.4 = (f32[520,128]{1,0:T(8,128)S(1)}, f32[520,128]{1,0:T(8,128)S(1)}, u32[]{:S(2)}, u32[]{:S(2)}) collective-permute-start(f32[520,128]{1,0:T(8,128)S(1)} %get-tuple-element.18), channel_id=1, source_target_pairs={{0,16},{8,72},{16,32},{24,88},{32,48},{40,104},{48,0},{56,120},{64... | collective-permute-start | bytes 798728 | tf_op jit(solution)/shard_map/ppermute | solution.py:345
  17.8 8.6 %collective-permute-start.6 = (f32[520,128]{1,0:T(8,128)S(1)}, f32[520,128]{1,0:T(8,128)S(1)}, u32[]{:S(2)}, u32[]{:S(2)}) collective-permute-start(f32[520,128]{1,0:T(8,128)S(1)} %get-tuple-element.17), channel_id=1, source_target_pairs={{0,48},{8,200},{16,0},{24,216},{32,16},{40,232},{48,32},{56,248},{... | collective-permute-start | bytes 798728 | tf_op jit(solution)/shard_map/ppermute | solution.py:345
  26.9 5.5 %collective-permute-start.7 = (f32[8,32,128]{2,1,0:T(8,128)S(1)}, f32[8,32,128]{2,1,0:T(8,128)S(1)}, u32[]{:S(2)}, u32[]{:S(2)}) collective-permute-start(f32[8,32,128]{2,1,0:T(8,128)S(1)} %get-tuple-element.25), channel_id=1, source_target_pairs={{0,128},{8,40},{16,144},{24,56},{32,160},{40,8},{48,176},{56,24},{... | collective-permute-start | bytes 393224 | tf_op jit(solution)/shard_map/ppermute | solution.py:352
  28.3 5.8 %collective-permute-start.8 = (f32[8,32,128]{2,1,0:T(8,128)S(1)}, f32[8,32,128]{2,1,0:T(8,128)S(1)}, u32[]{:S(2)}, u32[]{:S(2)}) collective-permute-start(f32[8,32,128]{2,1,0:T(8,128)S(1)} %get-tuple-element.27), channel_id=1, source_target_pairs={{0,64},{8,24},{16,80},{24,40},{32,96},{40,56},{48,112},{56,8},{64,... | collective-permute-start | bytes 393224 | tf_op jit(solution)/shard_map/ppermute | solution.py:352
  28.7 5.4 %collective-permute-start.9 = (f32[8,32,128]{2,1,0:T(8,128)S(1)}, f32[8,32,128]{2,1,0:T(8,128)S(1)}, u32[]{:S(2)}, u32[]{:S(2)}) collective-permute-start(f32[8,32,128]{2,1,0:T(8,128)S(1)} %get-tuple-element.26), channel_id=1, source_target_pairs={{0,192},{8,56},{16,208},{24,8},{32,224},{40,24},{48,240},{56,40},{... | collective-permute-start | bytes 393224 | tf_op jit(solution)/shard_map/ppermute | solution.py:352
  53.2 3.2 %collective-permute-start.10 = (f32[32,128]{1,0:T(8,128)S(1)}, f32[32,128]{1,0:T(8,128)S(1)}, u32[]{:S(2)}, u32[]{:S(2)}) collective-permute-start(f32[32,128]{1,0:T(8,128)S(1)} %reduce_sum.9), channel_id=1, source_target_pairs={{0,8},{8,0},{16,24},{24,16},{32,40},{40,32},{48,56},{56,48},{64,72... | collective-permute-start | bytes 49160 | tf_op jit(solution)/shard_map/ppermute | solution.py:357
where the time goes:
time: 57.3 us; the launch traced here: 57.1 us
  blocking collectives  19.1 us (33%)
  starting transfers between devices  14.2 us (25%)
  waiting for transfers between devices  11.8 us (21%)
  Pallas kernels  10.1 us (18%)
  other arithmetic  1.61 us (3%)
    all_to_all x1, blocking collectives, local(): lax.all_to_all(row, ('fit', 'batch'), 0, 0, axis_index_groups=last_groups())  19.1 us
    pallas_call x1, Pallas kernels, grams(): pl.pallas_call(gram_kernel, in_specs=[hbm, pl.BlockSpec(memory_space=pl.A...  9.59 us
    ppermute x3, waiting for transfers between devices, local(): moved = [lax.ppermute(chip[u], 'fit', ring_moves(u, 0)) for u in (2, 1, 3)]  6.23 us
    ppermute x3, starting transfers between devices, local(): row = row + lax.ppermute(line[w], 'fit', ring_moves(w, 1))  4.02 us
    ppermute x3, starting transfers between devices, local(): moved = [lax.ppermute(chip[u], 'fit', ring_moves(u, 0)) for u in (2, 1, 3)]  3.95 us
    ppermute x4, starting transfers between devices, local(): lax.ppermute(send[u], 'fit', swap)  3.93 us
    ppermute x3, waiting for transfers between devices, local(): row = row + lax.ppermute(line[w], 'fit', ring_moves(w, 1))  3.09 us
    ppermute x1, starting transfers between devices, local(): other = lax.ppermute(mine, 'fit', swap)  2.34 us
  transfers between devices with their start and end apart: 11, of which 9 were waited for; matrix products, arithmetic and copies ran while one was open for 0% of the time, Pallas kernels for 0%

commit v1 on v0

--- a/solution.py
+++ b/solution.py
@@ -341,7 +341,11 @@
     parts = grams(half_ints, domain_tiles, tile_counts).reshape(CORES, RING, SHARE, TILE)
     keep, send = parts[0], parts[1]
     swap = [(f, f ^ 1) for f in range(RING * RING * CORES)]
-    chip = {u: keep[u] + lax.ppermute(send[u], "fit", swap) for u in (2, 1, 3, 0)}
+    arrived = {u: lax.ppermute(send[u], "fit", swap) for u in (2, 1, 3, 0)}
+    chip = {2: keep[2] + arrived[2]}
+    for before, u in ((2, 1), (1, 3), (3, 0)):
+        chip[before], ready = lax.optimization_barrier((chip[before], arrived[u]))
+        chip[u] = keep[u] + ready
     moved = [lax.ppermute(chip[u], "fit", ring_moves(u, 0)) for u in (2, 1, 3)]
     fit = lax.axis_index("fit")
     core = fit & 1

time: 57.3 us -> 57.8 us (level)
  blocking collectives: 19.1 us -> 18 us
  waiting for transfers between devices: 11.8 us -> 12.8 us
  starting transfers between devices: 14.2 us -> 14.8 us
    ppermute x3, waiting for transfers between devices: 6.23 us -> 7.85 us  [local(): moved = [lax.ppermute(chip[u], 'fit', ring_moves(u, 0)) for u in (2, 1, 3)]]
    ppermute x3, starting transfers between devices: 3.95 us -> 2.48 us  [local(): moved = [lax.ppermute(chip[u], 'fit', ring_moves(u, 0)) for u in (2, 1, 3)]]
    ppermute x3, starting transfers between devices: 4.02 us -> 5.38 us  [local(): row = row + lax.ppermute(line[w], 'fit', ring_moves(w, 1))]
    all_to_all x1, blocking collectives: 19.1 us -> 18 us  [local(): lax.all_to_all(row, ('fit', 'batch'), 0, 0, axis_index_groups=last_groups())]
    ppermute x1, starting transfers between devices: 2.34 us -> 3.05 us  [local(): other = lax.ppermute(mine, 'fit', swap)]
  transfers between devices with their start and end apart: 11 -> 11, of which waited for: 9 -> 8; matrix products, arithmetic and copies ran while one was open for 0% -> 0% of each run, Pallas kernels for 0% -> 0%
where the time goes in v1:
time: 57.8 us; the launch traced here: 57.6 us
  blocking collectives  18 us (31%)
  starting transfers between devices  14.8 us (26%)
  waiting for transfers between devices  12.8 us (22%)
  Pallas kernels  10.1 us (17%)
  other arithmetic  1.6 us (3%)
    all_to_all x1, blocking collectives, local(): lax.all_to_all(row, ('fit', 'batch'), 0, 0, axis_index_groups=last_groups())  18 us
    pallas_call x1, Pallas kernels, grams(): pl.pallas_call(gram_kernel, in_specs=[hbm, pl.BlockSpec(memory_space=pl.A...  9.59 us
    ppermute x3, waiting for transfers between devices, local(): moved = [lax.ppermute(chip[u], 'fit', ring_moves(u, 0)) for u in (2, 1, 3)]  7.85 us
    ppermute x3, starting transfers between devices, local(): row = row + lax.ppermute(line[w], 'fit', ring_moves(w, 1))  5.38 us
    ppermute x4, starting transfers between devices, local(): arrived = {u: lax.ppermute(send[u], 'fit', swap) for u in (2, 1, 3, 0)}  3.93 us
    ppermute x1, starting transfers between devices, local(): other = lax.ppermute(mine, 'fit', swap)  3.05 us
    ppermute x3, waiting for transfers between devices, local(): row = row + lax.ppermute(line[w], 'fit', ring_moves(w, 1))  2.65 us
    ppermute x3, starting transfers between devices, local(): moved = [lax.ppermute(chip[u], 'fit', ring_moves(u, 0)) for u in (2, 1, 3)]  2.48 us
  transfers between devices with their start and end apart: 11, of which 8 were waited for; matrix products, arithmetic and copies ran while one was open for 0% of the time, Pallas kernels for 0%

profile of v1, /device:TPU:1, one launch (start us, length us, event | category | flops | bytes accessed | tf_op | source)
XLA Modules:
  0.0 57.6 jit_solution(11408905159716254197)
XLA Ops:
  0.0 0.7 %add_bitcast_fusion.slots_hbm = s32[6,32]{1,0:T(8,128)S(1)} fusion(s32[32,6]{0,1:T(8,128)} %param.5, s32[32,6]{0,1:T(8,128)} %param.4), kind=kLoop, calls=%fused_computation.18 | loop fusion | flops 384 | bytes 2304 | tf_op jit(solution)/shard_map/transpose | solution.py:215
  0.7 9.6 %grams.1 = f32[520,8,128]{2,1,0:T(8,128)S(1)} custom-call(s32[6,32]{1,0:T(8,128)S(1)} %add_bitcast_fusion.slots_hbm, bf16[960,48,128]{2,1,0:T(8,128)(2,1)} %x_hbm.1), custom_call_target="tpu_custom_call" | custom-call | tf_op jit(solution)/shard_map/grams/pallas_call | solution.py:195
  10.3 0.1 slice_bitcast_fusion
  10.4 3.3 %collective-permute-start = (f32[520,128]{1,0:T(8,128)S(1)}, f32[520,128]{1,0:T(8,128)S(1)}, u32[]{:S(2)}, u32[]{:S(2)}) collective-permute-start(f32[520,128]{1,0:T(8,128)S(1)} %get-tuple-element.32), channel_id=1, source_target_pairs={{0,8},{8,0},{16,24},{24,16},{32,40},{40,32},{48,56},{56,48},{64,72... | collective-permute-start | bytes 798728 | tf_op jit(solution)/shard_map/ppermute | solution.py:344
  13.7 0.1 collective-permute-start.1
  13.8 0.4 collective-permute-start.2
  14.2 0.1 collective-permute-start.3
  14.3 0.6 collective-permute-done
  14.9 0.1 fusion
  14.9 0.3 collective-permute-done.1
  15.3 0.3 collective-permute-done.2
  15.7 0.3 collective-permute-done.3
  16.0 0.7 %collective-permute-start.6 = (f32[520,128]{1,0:T(8,128)S(1)}, f32[520,128]{1,0:T(8,128)S(1)}, u32[]{:S(2)}, u32[]{:S(2)}) collective-permute-start(f32[520,128]{1,0:T(8,128)S(1)} %fusion.2), channel_id=1, source_target_pairs={{0,48},{8,200},{16,0},{24,216},{32,16},{40,232},{48,32},{56,248},{... | collective-permute-start | bytes 798728 | tf_op jit(solution)/shard_map/ppermute | solution.py:349
  16.8 0.7 %collective-permute-start.5 = (f32[520,128]{1,0:T(8,128)S(1)}, f32[520,128]{1,0:T(8,128)S(1)}, u32[]{:S(2)}, u32[]{:S(2)}) collective-permute-start(f32[520,128]{1,0:T(8,128)S(1)} %fusion.1), channel_id=1, source_target_pairs={{0,16},{8,72},{16,32},{24,88},{32,48},{40,104},{48,0},{56,120},{64... | collective-permute-start | bytes 798728 | tf_op jit(solution)/shard_map/ppermute | solution.py:349
  17.5 1.0 %collective-permute-start.4 = (f32[520,128]{1,0:T(8,128)S(1)}, f32[520,128]{1,0:T(8,128)S(1)}, u32[]{:S(2)}, u32[]{:S(2)}) collective-permute-start(f32[520,128]{1,0:T(8,128)S(1)} %fusion), channel_id=1, source_target_pairs={{0,32},{8,136},{16,48},{24,152},{32,0},{40,168},{48,16},{56,184},{... | collective-permute-start | bytes 798728 | tf_op jit(solution)/shard_map/ppermute | solution.py:349
  18.5 3.0 %collective-permute-done.6.three_ref = f32[520,128]{1,0:T(8,128)S(1)} collective-permute-done((f32[520,128]{1,0:T(8,128)S(1)}, f32[520,128]{1,0:T(8,128)S(1)}, u32[]{:S(2)}, u32[]{:S(2)}) %collective-permute-start.6) | collective-permute-done | bytes 266272 | tf_op jit(solution)/shard_map/ppermute | solution.py:349
  21.6 4.8 %collective-permute-done.5.two_ref = f32[520,128]{1,0:T(8,128)S(1)} collective-permute-done((f32[520,128]{1,0:T(8,128)S(1)}, f32[520,128]{1,0:T(8,128)S(1)}, u32[]{:S(2)}, u32[]{:S(2)}) %collective-permute-start.5) | collective-permute-done | bytes 266272 | tf_op jit(solution)/shard_map/ppermute | solution.py:349
  26.4 0.0 collective-permute-done.4.one_ref
  26.4 0.5 expand.1
  26.9 2.7 %collective-permute-start.7 = (f32[8,32,128]{2,1,0:T(8,128)S(1)}, f32[8,32,128]{2,1,0:T(8,128)S(1)}, u32[]{:S(2)}, u32[]{:S(2)}) collective-permute-start(f32[8,32,128]{2,1,0:T(8,128)S(1)} %get-tuple-element.33), channel_id=1, source_target_pairs={{0,128},{8,40},{16,144},{24,56},{32,160},{40,8},{48,176},{56,24},{... | collective-permute-start | bytes 393224 | tf_op jit(solution)/shard_map/ppermute | solution.py:356
  29.6 0.4 collective-permute-start.8
  30.0 2.3 %collective-permute-start.9 = (f32[8,32,128]{2,1,0:T(8,128)S(1)}, f32[8,32,128]{2,1,0:T(8,128)S(1)}, u32[]{:S(2)}, u32[]{:S(2)}) collective-permute-start(f32[8,32,128]{2,1,0:T(8,128)S(1)} %get-tuple-element.34), channel_id=1, source_target_pairs={{0,192},{8,56},{16,208},{24,8},{32,224},{40,24},{48,240},{56,40},{... | collective-permute-start | bytes 393224 | tf_op jit(solution)/shard_map/ppermute | solution.py:356
  32.3 0.0 collective-permute-done.7
  32.3 2.6 %collective-permute-done.8 = f32[8,32,128]{2,1,0:T(8,128)S(1)} collective-permute-done((f32[8,32,128]{2,1,0:T(8,128)S(1)}, f32[8,32,128]{2,1,0:T(8,128)S(1)}, u32[]{:S(2)}, u32[]{:S(2)}) %collective-permute-start.8) | collective-permute-done | bytes 131104 | tf_op jit(solution)/shard_map/ppermute | solution.py:356
  34.9 0.0 collective-permute-done.9
  35.0 18.0 %all_to_all.5 = f32[8,32,128]{2,1,0:T(8,128)S(1)} all-to-all(f32[8,32,128]{2,1,0:T(8,128)S(1)} %fusion.5), channel_id=1, replica_groups={{0,33,2,35,4,37,6,39},{16,49,18,51,20,53,22,55},{32,1,34,3,36,5,38,7},{..., dimensions={0} | all-to-all | bytes 262144 | tf_op jit(solution)/shard_map/all_to_all | solution.py:358
  53.0 3.1 %collective-permute-start.10 = (f32[32,128]{1,0:T(8,128)S(1)}, f32[32,128]{1,0:T(8,128)S(1)}, u32[]{:S(2)}, u32[]{:S(2)}) collective-permute-start(f32[32,128]{1,0:T(8,128)S(1)} %reduce_sum.9), channel_id=1, source_target_pairs={{0,8},{8,0},{16,24},{24,16},{32,40},{40,32},{48,56},{56,48},{64,72... | collective-permute-start | bytes 49160 | tf_op jit(solution)/shard_map/ppermute | solution.py:361
  56.0 0.1 fusion.10
  56.1 0.8 %collective-permute-done.10 = f32[32,128]{1,0:T(8,128)S(1)} collective-permute-done((f32[32,128]{1,0:T(8,128)S(1)}, f32[32,128]{1,0:T(8,128)S(1)}, u32[]{:S(2)}, u32[]{:S(2)}) %collective-permute-start.10) | collective-permute-done | bytes 16416 | tf_op jit(solution)/shard_map/ppermute | solution.py:361
  56.9 0.1 fusion.9
  56.9 0.7 %fusion.6 = f32[32,128]{1,0:T(8,128)} fusion(f32[32,128]{1,0:T(8,128)S(1)} %reduce_sum.9, f32[32,64]{1,0:T(8,128)S(1)} %get-tuple-element.39, f32[32,64]{1,0:T(8,128)S(1)} %get-tuple-element.38, f32[32,128]{1,0:T(8,128)S(1)} %collective-permute-done.10, f32[32,64]{1,0:T(8,128)S(1)} %get-tuple-element.37, f32[32,64]{1,0:T(8,128)S(1)} %get-tuple-element.36, ...), kind=kLoop, calls=%fused_computation.16 | loop fusion | flops 20480 | bytes 82049 | tf_op jit(solution)/shard_map/jit(_where)/select_n | solution.py:364
  (7 shorter events, 0.2 us)
Async XLA Ops:
  10.4 4.5 %collective-permute-start = (f32[520,128]{1,0:T(8,128)S(1)}, f32[520,128]{1,0:T(8,128)S(1)}, u32[]{:S(2)}, u32[]{:S(2)}) collective-permute-start(f32[520,128]{1,0:T(8,128)S(1)} %get-tuple-element.32), channel_id=1, source_target_pairs={{0,8},{8,0},{16,24},{24,16},{32,40},{40,32},{48,56},{56,48},{64,72... | collective-permute-start | bytes 798728 | tf_op jit(solution)/shard_map/ppermute | solution.py:344
  13.7 1.5 %collective-permute-start.1 = (f32[520,128]{1,0:T(8,128)S(1)}, f32[520,128]{1,0:T(8,128)S(1)}, u32[]{:S(2)}, u32[]{:S(2)}) collective-permute-start(f32[520,128]{1,0:T(8,128)S(1)} %get-tuple-element.31), channel_id=1, source_target_pairs={{0,8},{8,0},{16,24},{24,16},{32,40},{40,32},{48,56},{56,48},{64,72... | collective-permute-start | bytes 798728 | tf_op jit(solution)/shard_map/ppermute | solution.py:344
  13.8 1.8 %collective-permute-start.2 = (f32[520,128]{1,0:T(8,128)S(1)}, f32[520,128]{1,0:T(8,128)S(1)}, u32[]{:S(2)}, u32[]{:S(2)}) collective-permute-start(f32[520,128]{1,0:T(8,128)S(1)} %get-tuple-element.30), channel_id=1, source_target_pairs={{0,8},{8,0},{16,24},{24,16},{32,40},{40,32},{48,56},{56,48},{64,72... | collective-permute-start | bytes 798728 | tf_op jit(solution)/shard_map/ppermute | solution.py:344
  14.2 1.8 %collective-permute-start.3 = (f32[520,128]{1,0:T(8,128)S(1)}, f32[520,128]{1,0:T(8,128)S(1)}, u32[]{:S(2)}, u32[]{:S(2)}) collective-permute-start(f32[520,128]{1,0:T(8,128)S(1)} %get-tuple-element.29), channel_id=1, source_target_pairs={{0,8},{8,0},{16,24},{24,16},{32,40},{40,32},{48,56},{56,48},{64,72... | collective-permute-start | bytes 798728 | tf_op jit(solution)/shard_map/ppermute | solution.py:344
  16.0 5.6 %collective-permute-start.6 = (f32[520,128]{1,0:T(8,128)S(1)}, f32[520,128]{1,0:T(8,128)S(1)}, u32[]{:S(2)}, u32[]{:S(2)}) collective-permute-start(f32[520,128]{1,0:T(8,128)S(1)} %fusion.2), channel_id=1, source_target_pairs={{0,48},{8,200},{16,0},{24,216},{32,16},{40,232},{48,32},{56,248},{... | collective-permute-start | bytes 798728 | tf_op jit(solution)/shard_map/ppermute | solution.py:349
  16.8 9.6 %collective-permute-start.5 = (f32[520,128]{1,0:T(8,128)S(1)}, f32[520,128]{1,0:T(8,128)S(1)}, u32[]{:S(2)}, u32[]{:S(2)}) collective-permute-start(f32[520,128]{1,0:T(8,128)S(1)} %fusion.1), channel_id=1, source_target_pairs={{0,16},{8,72},{16,32},{24,88},{32,48},{40,104},{48,0},{56,120},{64... | collective-permute-start | bytes 798728 | tf_op jit(solution)/shard_map/ppermute | solution.py:349
  17.5 8.9 %collective-permute-start.4 = (f32[520,128]{1,0:T(8,128)S(1)}, f32[520,128]{1,0:T(8,128)S(1)}, u32[]{:S(2)}, u32[]{:S(2)}) collective-permute-start(f32[520,128]{1,0:T(8,128)S(1)} %fusion), channel_id=1, source_target_pairs={{0,32},{8,136},{16,48},{24,152},{32,0},{40,168},{48,16},{56,184},{... | collective-permute-start | bytes 798728 | tf_op jit(solution)/shard_map/ppermute | solution.py:349
  26.9 5.4 %collective-permute-start.7 = (f32[8,32,128]{2,1,0:T(8,128)S(1)}, f32[8,32,128]{2,1,0:T(8,128)S(1)}, u32[]{:S(2)}, u32[]{:S(2)}) collective-permute-start(f32[8,32,128]{2,1,0:T(8,128)S(1)} %get-tuple-element.33), channel_id=1, source_target_pairs={{0,128},{8,40},{16,144},{24,56},{32,160},{40,8},{48,176},{56,24},{... | collective-permute-start | bytes 393224 | tf_op jit(solution)/shard_map/ppermute | solution.py:356
  29.6 5.3 %collective-permute-start.8 = (f32[8,32,128]{2,1,0:T(8,128)S(1)}, f32[8,32,128]{2,1,0:T(8,128)S(1)}, u32[]{:S(2)}, u32[]{:S(2)}) collective-permute-start(f32[8,32,128]{2,1,0:T(8,128)S(1)} %get-tuple-element.35), channel_id=1, source_target_pairs={{0,64},{8,24},{16,80},{24,40},{32,96},{40,56},{48,112},{56,8},{64,... | collective-permute-start | bytes 393224 | tf_op jit(solution)/shard_map/ppermute | solution.py:356
  30.0 4.9 %collective-permute-start.9 = (f32[8,32,128]{2,1,0:T(8,128)S(1)}, f32[8,32,128]{2,1,0:T(8,128)S(1)}, u32[]{:S(2)}, u32[]{:S(2)}) collective-permute-start(f32[8,32,128]{2,1,0:T(8,128)S(1)} %get-tuple-element.34), channel_id=1, source_target_pairs={{0,192},{8,56},{16,208},{24,8},{32,224},{40,24},{48,240},{56,40},{... | collective-permute-start | bytes 393224 | tf_op jit(solution)/shard_map/ppermute | solution.py:356
  53.0 3.9 %collective-permute-start.10 = (f32[32,128]{1,0:T(8,128)S(1)}, f32[32,128]{1,0:T(8,128)S(1)}, u32[]{:S(2)}, u32[]{:S(2)}) collective-permute-start(f32[32,128]{1,0:T(8,128)S(1)} %reduce_sum.9), channel_id=1, source_target_pairs={{0,8},{8,0},{16,24},{24,16},{32,40},{40,32},{48,56},{56,48},{64,72... | collective-permute-start | bytes 49160 | tf_op jit(solution)/shard_map/ppermute | solution.py:361
